TPU v7x, 128 devices: a whole 4x4x4 slice. The times are simulated.
128 devices in a mesh: mom: 8 (over y, core), pair: 16 (over x, z).
Axes of the slice: x: 4, y: 4, z: 4, core: 2. Of those that a mesh axis runs over, the one named last changes fastest.
Arguments:
- blocks: bfloat16 [8, 16, 1024, 1024], P('mom', None, 'pair'), may hold values from -1.078125 to 1.078125
- left_ids: int32 [8, 48], P('mom', 'pair'), may hold values from 0 to 15
- right_ids: int32 [8, 48], P('mom', 'pair'), may hold values from 0 to 15
- slice_ids: int32 [8, 48], P('mom', 'pair'), may hold values from 0 to 1
- weight_ids: int32 [8, 48], P('mom', 'pair'), may hold values from 0 to 7
- counts: int32 [8, 16], P('mom', 'pair'), may hold values from 1 to 3, 32 in all within a row
- subduction: float32 [8], replicated, may hold values from -1 to 1
Outputs:
- operator: float32 [8, 1024, 2, 1024], P('mom', 'pair')
Inputs may be any that keep to these rules, and one draw needn't show every extreme that they name: Each row of counts sums to exactly 32.
All inputs are finite; a program needn't handle non-finite values. No bound on the sum of `counts` on one device may be relied on, other than what follows from the above.
Results may differ from a plain program's by a relative error of at most 0.0029.
Values may be sent and summed in bfloat16 or wider, within the bound.
A program may use at most 128 MiB of HBM per device.

v0:
```python
import jax
import jax.numpy as jnp
from jax import lax
from jax.sharding import PartitionSpec as P

PAIR_DEV = 3
SLICES = 2


def partner_2(shard, axis, apart):
    return lax.ppermute(shard, axis, [(i, i ^ 1 << apart) for i in range(lax.axis_size(axis))])


def mixing_table(lefts, rights, slices, weights, allowed, subduction, families):
    total_slots = lefts.shape[0]
    slot = jnp.arange(total_slots, dtype=jnp.int32)
    list_of = slot // PAIR_DEV
    lists = jnp.arange(allowed.shape[0], dtype=jnp.int32)
    limit = jnp.sum(jnp.where(list_of[:, None] == lists[None, :], allowed[None, :], 0), axis=1)
    live = slot % PAIR_DEV < limit
    table_ids = jnp.arange(subduction.shape[0], dtype=jnp.int32)
    looked = jnp.sum(
        jnp.where(weights[:, None] == table_ids[None, :], subduction[None, :], 0.0), axis=1
    )
    select = (slices[:, None] == jnp.arange(SLICES, dtype=jnp.int32)[None, :]).astype(jnp.float32)
    scales = jnp.where(live, looked, 0.0)[:, None] * select
    fam_ids = jnp.arange(families, dtype=jnp.int32)
    right_hot = (rights[:, None] == fam_ids[None, :]).astype(jnp.float32)
    left_hot = (lefts[:, None] == fam_ids[None, :]).astype(jnp.float32)
    return jnp.einsum("kt,kb,ka->tba", scales, right_hot, left_hot, precision=lax.Precision.HIGHEST)


def combine_left(mixing, panels):
    families = panels.shape[0]
    flat = panels.astype(jnp.float32).reshape(families, -1)
    mixed = jnp.dot(
        mixing.reshape(SLICES * families, families), flat, precision=lax.Precision.HIGHEST
    )
    return mixed.astype(jnp.bfloat16).reshape((SLICES, families) + panels.shape[1:])


def body(blocks, left_ids, right_ids, slice_ids, weight_ids, counts, subduction):
    gathered = (
        lax.all_gather(left_ids, "pair", axis=1, tiled=True),
        lax.all_gather(right_ids, "pair", axis=1, tiled=True),
        lax.all_gather(slice_ids, "pair", axis=1, tiled=True),
        lax.all_gather(weight_ids, "pair", axis=1, tiled=True),
        lax.all_gather(counts, "pair", axis=1, tiled=True),
    )
    own = blocks[0]
    families = own.shape[0]
    mixing = mixing_table(
        gathered[0][0],
        gathered[1][0],
        gathered[2][0],
        gathered[3][0],
        gathered[4][0],
        subduction,
        families,
    )
    partner = partner_2(own, "mom", 0)
    combined = combine_left(mixing, own)
    result = jnp.einsum(
        "tbij,bjl->itl",
        combined,
        lax.all_gather(partner, "pair", axis=1, tiled=True),
        preferred_element_type=jnp.float32,
    )
    return result.reshape((1,) + result.shape)


def solution(mesh):
    return jax.shard_map(
        body,
        mesh=mesh,
        in_specs=(
            P("mom", None, "pair", None),
            P("mom", "pair"),
            P("mom", "pair"),
            P("mom", "pair"),
            P("mom", "pair"),
            P("mom", "pair"),
            P(),
        ),
        out_specs=P("mom", "pair", None, None),
        check_vma=False,
    )
```

profile of v0, /device:TPU:1, one launch (start us, length us, event | category | flops | bytes accessed | tf_op | source)
XLA Modules:
  0.0 235.2 jit_solution(4597328169797305027)
XLA Ops:
  6.5 0.0 copy-start.5
  6.6 0.0 all-gather.2.cloned.1.call-start
  6.6 1.5 collective-permute-start
  8.1 4.0 %collective-permute-done = bf16[16,64,1024]{2,1,0:T(8,128)(2,1)S(1)} collective-permute-done((bf16[16,64,1024]{2,1,0:T(8,128)(2,1)}, bf16[16,64,1024]{2,1,0:T(8,128)(2,1)S(1)}, u32[]{:S(2)}, u32[]{:S(2)}) %collective-permute-start) | collective-permute-done | bytes 2097184 | tf_op jit(solution)/shard_map/ppermute | solution.py:11
  12.1 1.3 copy-done
  13.4 0.0 all-gather.2.cloned.1.call-update
  14.1 2.7 %copy.11 = bf16[2,8,64,1024]{3,1,2,0:T(8,128)(2,1)S(1)} copy(bf16[2,8,64,1024]{3,2,1,0:T(8,128)(2,1)} %bitcast.49) | data formatting | bytes 4194304
  16.8 0.0 copy-done.6
  16.9 0.6 dynamic-slice
  18.1 0.7 bitcast_dynamic-update-slice_fusion.2
  18.8 0.0 copy-done.1
  18.8 0.1 bitcast_dynamic-update-slice_fusion.4
  18.9 0.1 bitcast_dynamic-update-slice_fusion.1
  19.0 0.1 bitcast_dynamic-update-slice_fusion.3
  19.1 0.1 bitcast_dynamic-update-slice_fusion
  19.2 13.6 %all-reduce.5 = (s32[48]{0:T(128)S(1)}, s32[48]{0:T(128)S(1)}, s32[16]{0:T(128)S(1)}, s32[48]{0:T(128)S(1)}, s32[48]{0:T(128)S(1)}) all-reduce(s32[48]{0:T(128)S(1)} %bitcast_dynamic-update-slice_fusion.3, s32[48]{0:T(128)S(1)} %bitcast_dynamic-update-slice_fusion.1, ...), channel_id=1, replica_groups=mesh['mom'=8,'pair'=16] {'pair'}, use_global_device_ids=true, to_apply=%add.1 | all-reduce | flops 208 | bytes 1664
  32.9 0.1 select_reduce_fusion.1
  32.9 0.1 select_reduce_fusion
  33.1 0.1 fusion.8
  33.2 3.6 %convolution_convert_fusion = bf16[32,65536]{1,0:T(8,128)(2,1)S(1)} fusion(f32[32,16]{1,0:T(8,128)S(1)} %bitcast.50, bf16[16,65536]{1,0:T(8,128)(2,1)S(1)} %bitcast.47), kind=kOutput, calls=%fused_computation | convolution fusion | flops 404750336 | bytes 6293504 | tf_op jit(solution)/shard_map/dot_general | solution.py:36
  36.8 4.4 %copy.12 = bf16[4,8,64,1024]{3,2,1,0:T(8,128)(2,1)} copy(bf16[4,8,64,1024]{3,1,2,0:T(8,128)(2,1)S(1)} %bitcast.46) | data formatting | bytes 8388608
  41.1 171.9 %all-gather.2.cloned.1.call-done = bf16[16,1024,1024]{2,1,0:T(8,128)(2,1)} async-done(((bf16[16,64,1024]{2,1,0:T(8,128)(2,1)}), bf16[16,1024,1024]{2,1,0:T(8,128)(2,1)}) %all-gather.2.cloned.1.call-update) | async-done | bytes 33554448 | tf_op jit(solution)/shard_map/all_gather | solution.py:66
  213.0 14.1 %fusion.3 = f32[1,64,2,1024]{3,1,2,0:T(8,128)S(1)} fusion(bf16[16,1024,1024]{2,1,0:T(8,128)(2,1)} %all-gather.2.cloned.1.call-done, bf16[2,16,64,1024]{3,2,1,0:T(8,128)(2,1)} %bitcast.45), kind=kOutput, calls=%fused_computation.4 | convolution fusion | flops 4294967296 | bytes 38273024 | tf_op jit(solution)/shard_map/tbij,bjl->itl/dot_general | solution.py:63
  227.1 1.2 copy.9
  (19 shorter events, 0.1 us)
Async XLA Ops:
  6.5 10.3 %copy-start.6 = (u32[128]{0:T(128)S(1)}, u32[128]{0:T(128)}, u32[]{:S(2)}) copy-start(u32[128]{0:T(128)} %constant.32) | copy-start | bytes 1540
  6.5 12.3 %copy-start.1 = (s32[1,3]{1,0:T(1,128)S(1)}, s32[1,3]{1,0:T(1,128)}, u32[]{:S(2)}) copy-start(s32[1,3]{1,0:T(1,128)} %param.9) | copy-start | bytes 40
  6.5 12.4 %copy-start.2 = (s32[1,3]{1,0:T(1,128)S(1)}, s32[1,3]{1,0:T(1,128)}, u32[]{:S(2)}) copy-start(s32[1,3]{1,0:T(1,128)} %param.11) | copy-start | bytes 40
  6.5 12.5 %copy-start.3 = (s32[1,3]{1,0:T(1,128)S(1)}, s32[1,3]{1,0:T(1,128)}, u32[]{:S(2)}) copy-start(s32[1,3]{1,0:T(1,128)} %param.10) | copy-start | bytes 40
  6.5 12.6 %copy-start.4 = (s32[1,3]{1,0:T(1,128)S(1)}, s32[1,3]{1,0:T(1,128)}, u32[]{:S(2)}) copy-start(s32[1,3]{1,0:T(1,128)} %param.8) | copy-start | bytes 40
  6.5 26.3 %copy-start.5 = (f32[8]{0:T(128)S(1)}, f32[8]{0:T(128)}, u32[]{:S(2)}) copy-start(f32[8]{0:T(128)} %param.13) | copy-start | bytes 100
  6.6 206.5 %all-gather.2.cloned.1.call-start = ((), (), s32[]{:S(2)}) async-start(), calls=%async_computation | async-start | bytes 35651584 | tf_op jit(solution)/shard_map/all_gather | solution.py:66
  6.6 5.5 %collective-permute-start = (bf16[16,64,1024]{2,1,0:T(8,128)(2,1)}, bf16[16,64,1024]{2,1,0:T(8,128)(2,1)S(1)}, u32[]{:S(2)}, u32[]{:S(2)}) collective-permute-start(bf16[16,64,1024]{2,1,0:T(8,128)(2,1)} %bitcast.48), channel_id=1, source_target_pairs={{0,16},{16,0},{32,48},{48,32},{64,80},{80,64},{96,112},{112,96},{1... | collective-permute-start | bytes 6291464 | tf_op jit(solution)/shard_map/ppermute | solution.py:11
  12.1 1.3 copy-start
Sparse Core Ops, SparseCore 0:
  13.6 199.4 all-gather.1
where the time goes:
time: 235 us
  waiting for transfers between devices  176 us (75%)
  matrix products  17.8 us (8%)
  between operations  14.8 us (6%)
  blocking collectives  13.6 us (6%)
  local copies, waits for them, and re-layouts  11.3 us (5%)
    all_gather x1, waiting for transfers between devices, body(): lax.all_gather(partner, 'pair', axis=1, tiled=True)  172 us
    dot_general x1, matrix products, body(): jnp.einsum('tbij,bjl->itl', combined, lax.all_gather(partner, 'pair', axi...  14.1 us
    unnamed x1, blocking collectives  13.6 us
    unnamed x27, local copies, waits for them, and re-layouts  10.1 us
  transfers between devices with their start and end apart: 2, of which 2 were waited for; matrix products, arithmetic and copies ran while one was open for 5% of the time, Pallas kernels for 0%

commit v1 on v0

--- a/solution.py
+++ b/solution.py
@@ -40,6 +40,32 @@
 
 
 def body(blocks, left_ids, right_ids, slice_ids, weight_ids, counts, subduction):
+
+    def _supply_all_squares(xx, d0):
+        local_next = lax.psum(1, "pair")
+        near, work_now, arr_next = (local_next, lax.axis_index("pair"), xx.shape[d0])
+        history = []
+        for w in [*range(near)]:
+            history.append((w, (w + 1) % near))
+        row_list = []
+        for w in tuple(range(near)):
+            row_list.append((w, (w - 1) % near))
+        last = jnp.zeros((*xx.shape[:d0], near * arr_next, *xx.shape[d0 + 1 :]), xx.dtype)
+        last = lax.dynamic_update_slice_in_dim(last, xx, work_now * arr_next, axis=d0)
+        part_now = low = xx
+        z_new = near // 2
+        for jj in tuple(range(1, z_new + 1)):
+            part_now = lax.ppermute(part_now, "pair", history)
+            last = lax.dynamic_update_slice_in_dim(
+                last, part_now, (work_now - jj) % near * arr_next, axis=d0
+            )
+            if jj < near - z_new:
+                low = lax.ppermute(low, "pair", row_list)
+                last = lax.dynamic_update_slice_in_dim(
+                    last, low, (work_now + jj) % near * arr_next, axis=d0
+                )
+        return last
+
     gathered = (
         lax.all_gather(left_ids, "pair", axis=1, tiled=True),
         lax.all_gather(right_ids, "pair", axis=1, tiled=True),
@@ -63,7 +89,7 @@
     result = jnp.einsum(
         "tbij,bjl->itl",
         combined,
-        lax.all_gather(partner, "pair", axis=1, tiled=True),
+        _supply_all_squares(partner, d0=1),
         preferred_element_type=jnp.float32,
     )
     return result.reshape((1,) + result.shape)

time: 235 us -> 442 us (1.88)
  the two profiles are of different devices: /device:TPU:1 before, /device:TPU:0 now
where the time goes in v1:
time: 442 us
  waiting for transfers between devices  272 us (62%)
  local copies, waits for them, and re-layouts  64.4 us (15%)
  blocking collectives  46.4 us (10%)
  starting transfers between devices  40.1 us (9%)
  matrix products  17 us (4%)
    ppermute x8, waiting for transfers between devices, _supply_all_squares(): part_now = lax.ppermute(part_now, 'pair', history)  257 us
    unnamed x1, blocking collectives  46.4 us
    ppermute x7, starting transfers between devices, _supply_all_squares(): low = lax.ppermute(low, 'pair', row_list)  38 us
    dynamic_update_slice x8, local copies, waits for them, and re-layouts, _supply_all_squares(): lax.dynamic_update_slice_in_dim(last, part_now, (work_now - jj) % near *...  16.6 us
    broadcast_in_dim x1, local copies, waits for them, and re-layouts, _supply_all_squares(): jnp.zeros((*xx.shape[:d0], near * arr_next, *xx.shape[d0 + 1:]), xx.dtype)  16.1 us
    unnamed x49, local copies, waits for them, and re-layouts  15.5 us
    dynamic_update_slice x7, local copies, waits for them, and re-layouts, _supply_all_squares(): lax.dynamic_update_slice_in_dim(last, low, (work_now + jj) % near * arr_n...  13.6 us
    dot_general x1, matrix products, body(): jnp.einsum('tbij,bjl->itl', combined, _supply_all_squares(partner, d0=1),...  13.3 us
  transfers between devices with their start and end apart: 16, of which 11 were waited for; matrix products, arithmetic and copies ran while one was open for 14% of the time, Pallas kernels for 0%

profile of v1, /device:TPU:0, one launch (start us, length us, event | category | flops | bytes accessed | tf_op | source)
XLA Modules:
  0.0 441.8 jit_solution(11896751669837824995)
XLA Ops:
  0.0 4.4 collective-permute-done
  6.4 4.3 collective-permute-start.2
  10.7 45.9 %collective-permute-done.1 = bf16[16,64,1024]{2,1,0:T(8,128)(2,1)S(1)} collective-permute-done((bf16[16,64,1024]{2,1,0:T(8,128)(2,1)S(1)}, bf16[16,64,1024]{2,1,0:T(8,128)(2,1)S(1)}, u32[]{:S(2)}, u32[]{:S(2)}) %collective-permute-start.1) | collective-permute-done | bytes 2097184 | tf_op jit(solution)/shard_map/ppermute | solution.py:58
  58.0 5.3 %collective-permute-start.4 = (bf16[16,64,1024]{2,1,0:T(8,128)(2,1)S(1)}, bf16[16,64,1024]{2,1,0:T(8,128)(2,1)S(1)}, u32[]{:S(2)}, u32[]{:S(2)}) collective-permute-start(bf16[16,64,1024]{2,1,0:T(8,128)(2,1)S(1)} %collective-permute-done.2), channel_id=1, source_target_pairs={{0,15},{1,0},{2,1},{3,2},{4,3},{5,4},{6,5},{7,6},{8,7},{9,8},{10,9... | collective-permute-start | bytes 6291464 | tf_op jit(solution)/shard_map/ppermute | solution.py:63
  63.3 43.8 %collective-permute-done.3 = bf16[16,64,1024]{2,1,0:T(8,128)(2,1)S(1)} collective-permute-done((bf16[16,64,1024]{2,1,0:T(8,128)(2,1)S(1)}, bf16[16,64,1024]{2,1,0:T(8,128)(2,1)S(1)}, u32[]{:S(2)}, u32[]{:S(2)}) %collective-permute-start.3) | collective-permute-done | bytes 2097184 | tf_op jit(solution)/shard_map/ppermute | solution.py:58
  108.5 5.0 %collective-permute-start.6 = (bf16[16,64,1024]{2,1,0:T(8,128)(2,1)S(1)}, bf16[16,64,1024]{2,1,0:T(8,128)(2,1)S(1)}, u32[]{:S(2)}, u32[]{:S(2)}) collective-permute-start(bf16[16,64,1024]{2,1,0:T(8,128)(2,1)S(1)} %collective-permute-done.4), channel_id=1, source_target_pairs={{0,15},{1,0},{2,1},{3,2},{4,3},{5,4},{6,5},{7,6},{8,7},{9,8},{10,9... | collective-permute-start | bytes 6291464 | tf_op jit(solution)/shard_map/ppermute | solution.py:63
  113.5 43.2 %collective-permute-done.5 = bf16[16,64,1024]{2,1,0:T(8,128)(2,1)S(1)} collective-permute-done((bf16[16,64,1024]{2,1,0:T(8,128)(2,1)S(1)}, bf16[16,64,1024]{2,1,0:T(8,128)(2,1)S(1)}, u32[]{:S(2)}, u32[]{:S(2)}) %collective-permute-start.5) | collective-permute-done | bytes 2097184 | tf_op jit(solution)/shard_map/ppermute | solution.py:58
  157.0 5.8 %collective-permute-start.8 = (bf16[16,64,1024]{2,1,0:T(8,128)(2,1)S(1)}, bf16[16,64,1024]{2,1,0:T(8,128)(2,1)S(1)}, u32[]{:S(2)}, u32[]{:S(2)}) collective-permute-start(bf16[16,64,1024]{2,1,0:T(8,128)(2,1)S(1)} %collective-permute-done.6), channel_id=1, source_target_pairs={{0,15},{1,0},{2,1},{3,2},{4,3},{5,4},{6,5},{7,6},{8,7},{9,8},{10,9... | collective-permute-start | bytes 6291464 | tf_op jit(solution)/shard_map/ppermute | solution.py:63
  162.8 42.6 %collective-permute-done.7 = bf16[16,64,1024]{2,1,0:T(8,128)(2,1)S(1)} collective-permute-done((bf16[16,64,1024]{2,1,0:T(8,128)(2,1)S(1)}, bf16[16,64,1024]{2,1,0:T(8,128)(2,1)S(1)}, u32[]{:S(2)}, u32[]{:S(2)}) %collective-permute-start.7) | collective-permute-done | bytes 2097184 | tf_op jit(solution)/shard_map/ppermute | solution.py:58
  206.7 4.5 %collective-permute-start.10 = (bf16[16,64,1024]{2,1,0:T(8,128)(2,1)S(1)}, bf16[16,64,1024]{2,1,0:T(8,128)(2,1)}, u32[]{:S(2)}, u32[]{:S(2)}) collective-permute-start(bf16[16,64,1024]{2,1,0:T(8,128)(2,1)S(1)} %collective-permute-done.8), channel_id=1, source_target_pairs={{0,15},{1,0},{2,1},{3,2},{4,3},{5,4},{6,5},{7,6},{8,7},{9,8},{10,9... | collective-permute-start | bytes 6291464 | tf_op jit(solution)/shard_map/ppermute | solution.py:63
  211.1 42.1 %collective-permute-done.9 = bf16[16,64,1024]{2,1,0:T(8,128)(2,1)} collective-permute-done((bf16[16,64,1024]{2,1,0:T(8,128)(2,1)S(1)}, bf16[16,64,1024]{2,1,0:T(8,128)(2,1)}, u32[]{:S(2)}, u32[]{:S(2)}) %collective-permute-start.9) | collective-permute-done | bytes 2097184 | tf_op jit(solution)/shard_map/ppermute | solution.py:58
  256.6 5.4 %collective-permute-start.12 = (bf16[16,64,1024]{2,1,0:T(8,128)(2,1)}, bf16[16,64,1024]{2,1,0:T(8,128)(2,1)}, u32[]{:S(2)}, u32[]{:S(2)}) collective-permute-start(bf16[16,64,1024]{2,1,0:T(8,128)(2,1)} %collective-permute-done.10), channel_id=1, source_target_pairs={{0,15},{1,0},{2,1},{3,2},{4,3},{5,4},{6,5},{7,6},{8,7},{9,8},{10,9... | collective-permute-start | bytes 6291464 | tf_op jit(solution)/shard_map/ppermute | solution.py:63
  266.8 33.5 %collective-permute-done.11 = bf16[16,64,1024]{2,1,0:T(8,128)(2,1)} collective-permute-done((bf16[16,64,1024]{2,1,0:T(8,128)(2,1)}, bf16[16,64,1024]{2,1,0:T(8,128)(2,1)}, u32[]{:S(2)}, u32[]{:S(2)}) %collective-permute-start.11) | collective-permute-done | bytes 2097184 | tf_op jit(solution)/shard_map/ppermute | solution.py:58
  301.1 46.4 %all-reduce.5 = (s32[48]{0:T(128)S(1)}, s32[48]{0:T(128)S(1)}, s32[16]{0:T(128)S(1)}, s32[48]{0:T(128)S(1)}, s32[48]{0:T(128)S(1)}) all-reduce(s32[48]{0:T(128)S(1)} %bitcast_dynamic-update-slice_fusion.3, s32[48]{0:T(128)S(1)} %bitcast_dynamic-update-slice_fusion.1, ...), channel_id=1, replica_groups=mesh['mom'=8,'pair'=16] {'pair'}, use_global_device_ids=true, to_apply=%add.1 | all-reduce | flops 208 | bytes 1664
  348.5 3.6 convolution_convert_fusion
  352.1 4.4 copy.12
  356.5 16.1 %broadcast_in_dim.41 = bf16[16,1024,1024]{2,1,0:T(8,128)(2,1)} broadcast(bf16[]{:T(256)} %constant.106.clone.1), dimensions={} | broadcast | bytes 33554432 | tf_op jit(solution)/shard_map/broadcast_in_dim | solution.py:53
  374.1 7.7 %collective-permute-start.14 = (bf16[16,64,1024]{2,1,0:T(8,128)(2,1)}, bf16[16,64,1024]{2,1,0:T(8,128)(2,1)S(1)}, u32[]{:S(2)}, u32[]{:S(2)}) collective-permute-start(bf16[16,64,1024]{2,1,0:T(8,128)(2,1)} %collective-permute-done.12), channel_id=1, source_target_pairs={{0,15},{1,0},{2,1},{3,2},{4,3},{5,4},{6,5},{7,6},{8,7},{9,8},{10,9... | collective-permute-start | bytes 6291464 | tf_op jit(solution)/shard_map/ppermute | solution.py:63
  393.7 3.1 constant_dynamic-update-slice_fusion.6
  399.9 3.1 constant_dynamic-update-slice_fusion.4
  406.1 3.1 constant_dynamic-update-slice_fusion.2
  409.2 9.8 %collective-permute-done.14 = bf16[16,64,1024]{2,1,0:T(8,128)(2,1)S(1)} collective-permute-done((bf16[16,64,1024]{2,1,0:T(8,128)(2,1)}, bf16[16,64,1024]{2,1,0:T(8,128)(2,1)S(1)}, u32[]{:S(2)}, u32[]{:S(2)}) %collective-permute-start.14) | collective-permute-done | bytes 2097184 | tf_op jit(solution)/shard_map/ppermute | solution.py:63
  420.4 5.4 %collective-permute-done.15 = bf16[16,64,1024]{2,1,0:T(8,128)(2,1)S(1)} collective-permute-done((bf16[16,64,1024]{2,1,0:T(8,128)(2,1)}, bf16[16,64,1024]{2,1,0:T(8,128)(2,1)S(1)}, u32[]{:S(2)}, u32[]{:S(2)}) %collective-permute-start.15) | collective-permute-done | bytes 2097184 | tf_op jit(solution)/shard_map/ppermute | solution.py:58
  427.3 13.3 %fusion.3 = f32[1,64,2,1024]{3,1,2,0:T(8,128)S(1)} fusion(bf16[16,1024,1024]{2,1,0:T(8,128)(2,1)} %constant_dynamic-update-slice_fusion, bf16[2,16,64,1024]{3,2,1,0:T(8,128)(2,1)} %bitcast.45), kind=kOutput, calls=%fused_computation.4 | convolution fusion | flops 4294967296 | bytes 38273024 | tf_op jit(solution)/shard_map/tbij,bjl->itl/dot_general | solution.py:89
  (85 shorter events, 38.5 us)
Async XLA Ops:
  0.0 4.4 collective-permute-start
  4.4 52.3 %copy-start.10 = (bf16[16,64,1024]{2,1,0:T(8,128)(2,1)}, bf16[16,64,1024]{2,1,0:T(8,128)(2,1)S(1)}, u32[]{:S(2)}) copy-start(bf16[16,64,1024]{2,1,0:T(8,128)(2,1)S(1)} %collective-permute-done) | copy-start | bytes 6291460
  4.4 52.2 %collective-permute-start.1 = (bf16[16,64,1024]{2,1,0:T(8,128)(2,1)S(1)}, bf16[16,64,1024]{2,1,0:T(8,128)(2,1)S(1)}, u32[]{:S(2)}, u32[]{:S(2)}) collective-permute-start(bf16[16,64,1024]{2,1,0:T(8,128)(2,1)S(1)} %collective-permute-done), channel_id=1, source_target_pairs={{0,1},{1,2},{2,3},{3,4},{4,5},{5,6},{6,7},{7,8},{8,9},{9,10},{10,1... | collective-permute-start | bytes 6291464 | tf_op jit(solution)/shard_map/ppermute | solution.py:58
  6.4 50.3 %collective-permute-start.2 = (bf16[16,64,1024]{2,1,0:T(8,128)(2,1)S(1)}, bf16[16,64,1024]{2,1,0:T(8,128)(2,1)S(1)}, u32[]{:S(2)}, u32[]{:S(2)}) collective-permute-start(bf16[16,64,1024]{2,1,0:T(8,128)(2,1)S(1)} %collective-permute-done), channel_id=1, source_target_pairs={{0,15},{1,0},{2,1},{3,2},{4,3},{5,4},{6,5},{7,6},{8,7},{9,8},{10,9... | collective-permute-start | bytes 6291464 | tf_op jit(solution)/shard_map/ppermute | solution.py:63
  56.6 100.4 %copy-start.6 = (bf16[16,64,1024]{2,1,0:T(8,128)(2,1)}, bf16[16,64,1024]{2,1,0:T(8,128)(2,1)S(1)}, u32[]{:S(2)}) copy-start(bf16[16,64,1024]{2,1,0:T(8,128)(2,1)S(1)} %collective-permute-done.1) | copy-start | bytes 6291460
  56.6 50.5 %collective-permute-start.3 = (bf16[16,64,1024]{2,1,0:T(8,128)(2,1)S(1)}, bf16[16,64,1024]{2,1,0:T(8,128)(2,1)S(1)}, u32[]{:S(2)}, u32[]{:S(2)}) collective-permute-start(bf16[16,64,1024]{2,1,0:T(8,128)(2,1)S(1)} %collective-permute-done.1), channel_id=1, source_target_pairs={{0,1},{1,2},{2,3},{3,4},{4,5},{5,6},{6,7},{7,8},{8,9},{9,10},{10,1... | collective-permute-start | bytes 6291464 | tf_op jit(solution)/shard_map/ppermute | solution.py:58
  58.0 49.7 %collective-permute-start.4 = (bf16[16,64,1024]{2,1,0:T(8,128)(2,1)S(1)}, bf16[16,64,1024]{2,1,0:T(8,128)(2,1)S(1)}, u32[]{:S(2)}, u32[]{:S(2)}) collective-permute-start(bf16[16,64,1024]{2,1,0:T(8,128)(2,1)S(1)} %collective-permute-done.2), channel_id=1, source_target_pairs={{0,15},{1,0},{2,1},{3,2},{4,3},{5,4},{6,5},{7,6},{8,7},{9,8},{10,9... | collective-permute-start | bytes 6291464 | tf_op jit(solution)/shard_map/ppermute | solution.py:63
  107.1 49.6 %collective-permute-start.5 = (bf16[16,64,1024]{2,1,0:T(8,128)(2,1)S(1)}, bf16[16,64,1024]{2,1,0:T(8,128)(2,1)S(1)}, u32[]{:S(2)}, u32[]{:S(2)}) collective-permute-start(bf16[16,64,1024]{2,1,0:T(8,128)(2,1)S(1)} %collective-permute-done.3), channel_id=1, source_target_pairs={{0,1},{1,2},{2,3},{3,4},{4,5},{5,6},{6,7},{7,8},{8,9},{9,10},{10,1... | collective-permute-start | bytes 6291464 | tf_op jit(solution)/shard_map/ppermute | solution.py:58
  108.5 48.2 %copy-start.4 = (bf16[16,64,1024]{2,1,0:T(8,128)(2,1)}, bf16[16,64,1024]{2,1,0:T(8,128)(2,1)S(1)}, u32[]{:S(2)}) copy-start(bf16[16,64,1024]{2,1,0:T(8,128)(2,1)S(1)} %collective-permute-done.4) | copy-start | bytes 6291460
  108.5 48.5 %collective-permute-start.6 = (bf16[16,64,1024]{2,1,0:T(8,128)(2,1)S(1)}, bf16[16,64,1024]{2,1,0:T(8,128)(2,1)S(1)}, u32[]{:S(2)}, u32[]{:S(2)}) collective-permute-start(bf16[16,64,1024]{2,1,0:T(8,128)(2,1)S(1)} %collective-permute-done.4), channel_id=1, source_target_pairs={{0,15},{1,0},{2,1},{3,2},{4,3},{5,4},{6,5},{7,6},{8,7},{9,8},{10,9... | collective-permute-start | bytes 6291464 | tf_op jit(solution)/shard_map/ppermute | solution.py:63
  156.7 48.7 %collective-permute-start.7 = (bf16[16,64,1024]{2,1,0:T(8,128)(2,1)S(1)}, bf16[16,64,1024]{2,1,0:T(8,128)(2,1)S(1)}, u32[]{:S(2)}, u32[]{:S(2)}) collective-permute-start(bf16[16,64,1024]{2,1,0:T(8,128)(2,1)S(1)} %collective-permute-done.5), channel_id=1, source_target_pairs={{0,1},{1,2},{2,3},{3,4},{4,5},{5,6},{6,7},{7,8},{8,9},{9,10},{10,1... | collective-permute-start | bytes 6291464 | tf_op jit(solution)/shard_map/ppermute | solution.py:58
  157.0 48.4 %copy-start.12 = (bf16[16,64,1024]{2,1,0:T(8,128)(2,1)}, bf16[16,64,1024]{2,1,0:T(8,128)(2,1)S(1)}, u32[]{:S(2)}) copy-start(bf16[16,64,1024]{2,1,0:T(8,128)(2,1)S(1)} %collective-permute-done.6) | copy-start | bytes 6291460
  157.0 48.4 %collective-permute-start.8 = (bf16[16,64,1024]{2,1,0:T(8,128)(2,1)S(1)}, bf16[16,64,1024]{2,1,0:T(8,128)(2,1)S(1)}, u32[]{:S(2)}, u32[]{:S(2)}) collective-permute-start(bf16[16,64,1024]{2,1,0:T(8,128)(2,1)S(1)} %collective-permute-done.6), channel_id=1, source_target_pairs={{0,15},{1,0},{2,1},{3,2},{4,3},{5,4},{6,5},{7,6},{8,7},{9,8},{10,9... | collective-permute-start | bytes 6291464 | tf_op jit(solution)/shard_map/ppermute | solution.py:63
  205.4 47.8 %collective-permute-start.9 = (bf16[16,64,1024]{2,1,0:T(8,128)(2,1)S(1)}, bf16[16,64,1024]{2,1,0:T(8,128)(2,1)}, u32[]{:S(2)}, u32[]{:S(2)}) collective-permute-start(bf16[16,64,1024]{2,1,0:T(8,128)(2,1)S(1)} %collective-permute-done.7), channel_id=1, source_target_pairs={{0,1},{1,2},{2,3},{3,4},{4,5},{5,6},{6,7},{7,8},{8,9},{9,10},{10,1... | collective-permute-start | bytes 6291464 | tf_op jit(solution)/shard_map/ppermute | solution.py:58
  206.7 56.7 %copy-start.16 = (bf16[16,64,1024]{2,1,0:T(8,128)(2,1)}, bf16[16,64,1024]{2,1,0:T(8,128)(2,1)S(1)}, u32[]{:S(2)}) copy-start(bf16[16,64,1024]{2,1,0:T(8,128)(2,1)S(1)} %collective-permute-done.8) | copy-start | bytes 6291460
  206.7 49.9 %collective-permute-start.10 = (bf16[16,64,1024]{2,1,0:T(8,128)(2,1)S(1)}, bf16[16,64,1024]{2,1,0:T(8,128)(2,1)}, u32[]{:S(2)}, u32[]{:S(2)}) collective-permute-start(bf16[16,64,1024]{2,1,0:T(8,128)(2,1)S(1)} %collective-permute-done.8), channel_id=1, source_target_pairs={{0,15},{1,0},{2,1},{3,2},{4,3},{5,4},{6,5},{7,6},{8,7},{9,8},{10,9... | collective-permute-start | bytes 6291464 | tf_op jit(solution)/shard_map/ppermute | solution.py:63
  253.2 47.1 %collective-permute-start.11 = (bf16[16,64,1024]{2,1,0:T(8,128)(2,1)}, bf16[16,64,1024]{2,1,0:T(8,128)(2,1)}, u32[]{:S(2)}, u32[]{:S(2)}) collective-permute-start(bf16[16,64,1024]{2,1,0:T(8,128)(2,1)} %collective-permute-done.9), channel_id=1, source_target_pairs={{0,1},{1,2},{2,3},{3,4},{4,5},{5,6},{6,7},{7,8},{8,9},{9,10},{10,1... | collective-permute-start | bytes 6291464 | tf_op jit(solution)/shard_map/ppermute | solution.py:58
  256.6 117.5 %collective-permute-start.12 = (bf16[16,64,1024]{2,1,0:T(8,128)(2,1)}, bf16[16,64,1024]{2,1,0:T(8,128)(2,1)}, u32[]{:S(2)}, u32[]{:S(2)}) collective-permute-start(bf16[16,64,1024]{2,1,0:T(8,128)(2,1)} %collective-permute-done.10), channel_id=1, source_target_pairs={{0,15},{1,0},{2,1},{3,2},{4,3},{5,4},{6,5},{7,6},{8,7},{9,8},{10,9... | collective-permute-start | bytes 6291464 | tf_op jit(solution)/shard_map/ppermute | solution.py:63
  300.3 82.9 %collective-permute-start.13 = (bf16[16,64,1024]{2,1,0:T(8,128)(2,1)}, bf16[16,64,1024]{2,1,0:T(8,128)(2,1)}, u32[]{:S(2)}, u32[]{:S(2)}) collective-permute-start(bf16[16,64,1024]{2,1,0:T(8,128)(2,1)} %collective-permute-done.11), channel_id=1, source_target_pairs={{0,1},{1,2},{2,3},{3,4},{4,5},{5,6},{6,7},{7,8},{8,9},{9,10},{10,1... | collective-permute-start | bytes 6291464 | tf_op jit(solution)/shard_map/ppermute | solution.py:58
  356.5 32.7 %copy-start.13 = (bf16[16,64,1024]{2,1,0:T(8,128)(2,1)S(1)}, bf16[16,64,1024]{2,1,0:T(8,128)(2,1)}, u32[]{:S(2)}) copy-start(bf16[16,64,1024]{2,1,0:T(8,128)(2,1)} %copy-done.12) | copy-start | bytes 6291460
  356.5 34.2 %copy-start.15 = (bf16[16,64,1024]{2,1,0:T(8,128)(2,1)S(1)}, bf16[16,64,1024]{2,1,0:T(8,128)(2,1)}, u32[]{:S(2)}) copy-start(bf16[16,64,1024]{2,1,0:T(8,128)(2,1)} %copy-done.14) | copy-start | bytes 6291460
  356.5 35.7 %copy-start.17 = (bf16[16,64,1024]{2,1,0:T(8,128)(2,1)S(1)}, bf16[16,64,1024]{2,1,0:T(8,128)(2,1)}, u32[]{:S(2)}) copy-start(bf16[16,64,1024]{2,1,0:T(8,128)(2,1)} %copy-done.16) | copy-start | bytes 6291460
  374.1 44.9 %collective-permute-start.14 = (bf16[16,64,1024]{2,1,0:T(8,128)(2,1)}, bf16[16,64,1024]{2,1,0:T(8,128)(2,1)S(1)}, u32[]{:S(2)}, u32[]{:S(2)}) collective-permute-start(bf16[16,64,1024]{2,1,0:T(8,128)(2,1)} %collective-permute-done.12), channel_id=1, source_target_pairs={{0,15},{1,0},{2,1},{3,2},{4,3},{5,4},{6,5},{7,6},{8,7},{9,8},{10,9... | collective-permute-start | bytes 6291464 | tf_op jit(solution)/shard_map/ppermute | solution.py:63
  383.3 42.6 %collective-permute-start.15 = (bf16[16,64,1024]{2,1,0:T(8,128)(2,1)}, bf16[16,64,1024]{2,1,0:T(8,128)(2,1)S(1)}, u32[]{:S(2)}, u32[]{:S(2)}) collective-permute-start(bf16[16,64,1024]{2,1,0:T(8,128)(2,1)} %collective-permute-done.13), channel_id=1, source_target_pairs={{0,1},{1,2},{2,3},{3,4},{4,5},{5,6},{6,7},{7,8},{8,9},{9,10},{10,1... | collective-permute-start | bytes 6291464 | tf_op jit(solution)/shard_map/ppermute | solution.py:58
  (10 other events, 172.2 us)
